TPU v7x, 512 devices: a whole 4x8x8 slice. The times are simulated.
512 devices in a mesh: shard: 128 (over z, y, core), rep: 4 (over x).
Axes of the slice: x: 4, y: 8, z: 8, core: 2. Of those that a mesh axis runs over, the one named last changes fastest.
Arguments:
- queries: bfloat16 [4, 128, 32, 128], P('rep', 'shard'), may hold values from -0.5 to 0.5
- candidates: int32 [4, 128, 64], P('rep', 'shard'), may hold values from 0 to 2047, all different within a row; in each aligned block of 128 rows (0 to 127, 128 to 255, ..., all dimensions but the last counted through in order) at most 8 rows name the same one
- codebook: bfloat16 [524288, 128], P(('shard', 'rep')), may hold values from -0.5 to 0.5
- bucket_weights: float32 [4], replicated, may hold values from -0.1 to 0.1
- centroid_ids: int32 [2048, 128], P('shard'), may hold values from 0 to 4095
- residual_codes: int32 [2048, 128, 128], P('shard'), may hold values from 0 to 3
- passage_lengths: int32 [2048], P('shard'), may hold values from 1 to 128, 196608 in all
Outputs:
- best_centroid: float32 [4, 128, 32], P('rep', 'shard')
- scores: float32 [4, 128, 64], P('rep', 'shard')
Inputs may be any that keep to these rules, and one draw needn't show every extreme that they name: `candidates`: each query names 64 different passages. Within the 128 queries of one index of rep, no passage is named by more than 8 queries, a bound that some block reaches. `passage_lengths`: some passage has all 128 slots live.
All inputs are finite; a program needn't handle non-finite values. No bound on the sum of `passage_lengths` on one device may be relied on, other than what follows from the above.
Results may differ from a plain program's by a relative error of at most 0.00045.
Values may be sent and summed in bfloat16 or wider, within the bound.
A program may use at most 64 MiB of HBM per device.

v0:
```python
import math

import jax
import jax.numpy as jnp
from jax import lax
from jax.sharding import PartitionSpec as P

FAR_BELOW = -1e30


def on_device(
    queries, candidates, codebook, bucket_weights, centroid_ids, residual_codes, passage_lengths
):
    feature_width = queries.shape[3]
    query_len = queries.shape[2]
    per_device = queries.shape[1]
    owner_index = lax.axis_index("shard")
    group_queries, group_cands = (
        lax.all_gather(queries, "shard", axis=1, tiled=True),
        lax.all_gather(candidates, "shard", axis=1, tiled=True),
    )
    group_queries = group_queries[0]
    group_cands = group_cands[0]
    group_size = group_queries.shape[0]
    shard_book = lax.all_gather(codebook, "rep", axis=0, tiled=True)
    token_rows = group_queries.reshape(group_size * query_len, feature_width)
    block_rows = math.gcd(token_rows.shape[0], 512)

    def best_block(row_block):
        scored = jnp.dot(row_block, shard_book.T, preferred_element_type=jnp.float32)
        return jnp.max(scored, axis=1)

    partial_best = lax.map(best_block, token_rows.reshape(-1, block_rows, feature_width)).reshape(
        group_size, query_len
    )
    pass_count, pass_len = centroid_ids.shape
    centre_rows = jnp.take(shard_book, centroid_ids.reshape(-1), axis=0).reshape(
        pass_count, pass_len, feature_width
    )
    residual = jnp.zeros(residual_codes.shape, jnp.float32)
    for bucket in range(bucket_weights.shape[0]):
        residual = residual + jnp.where(residual_codes == bucket, bucket_weights[bucket], 0.0)
    decoded = (centre_rows.astype(jnp.float32) + residual).astype(jnp.bfloat16)
    live_mask = jnp.arange(pass_len, dtype=jnp.int32)[None, :] < passage_lengths[:, None]
    flat_tokens = decoded.reshape(pass_count * pass_len, feature_width)
    block_queries = math.gcd(group_size, max(1, 512 // query_len))

    def dense_block(query_block):
        similar = jnp.dot(
            query_block.reshape(-1, feature_width),
            flat_tokens.T,
            preferred_element_type=jnp.float32,
        )
        similar = similar.reshape(block_queries, query_len, pass_count, pass_len)
        similar = jnp.where(live_mask[None, None], similar, FAR_BELOW)
        return jnp.sum(jnp.max(similar, axis=3), axis=1)

    score_table = lax.map(
        dense_block, group_queries.reshape(-1, block_queries, query_len, feature_width)
    ).reshape(group_size, pass_count)
    merged = lax.pmax(partial_best, "shard")
    own_best = lax.dynamic_slice_in_dim(merged, owner_index * per_device, per_device, 0)
    local_index = group_cands - owner_index * pass_count
    picked = jnp.sum(
        jnp.where(
            local_index[:, :, None] == jnp.arange(pass_count, dtype=jnp.int32)[None, None, :],
            score_table[:, None, :],
            0.0,
        ),
        axis=2,
    )
    own_scores = lax.psum_scatter(picked, "shard", scatter_dimension=0, tiled=True)
    return (own_best[None], own_scores[None])


def solution(mesh):
    in_specs = (
        P("rep", "shard", None, None),
        P("rep", "shard", None),
        P(("shard", "rep"), None),
        P(),
        P("shard", None),
        P("shard", None, None),
        P("shard"),
    )
    out_specs = (P("rep", "shard", None), P("rep", "shard", None))
    return jax.shard_map(
        on_device, mesh=mesh, in_specs=in_specs, out_specs=out_specs, check_vma=False
    )
```

profile of v0, /device:TPU:1, one launch (start us, length us, event | category | flops | bytes accessed | tf_op | source)
XLA Modules:
  0.0 1154.5 jit_solution(518266250836284800)
XLA Ops:
  7.2 0.7 all-gather.5.cloned.1.call-update
  7.9 0.7 all-gather.3.cloned.1.call-update
  8.7 51.9 %all_gather.11 = s32[1,128,64]{2,0,1:T(1,128)S(1)} all-gather(s32[1,1,64]{2,0,1:T(1,128)} %bitcast.62), channel_id=1, replica_groups=mesh['shard'=128,'rep'=4] {'shard'}, dimensions={1}, use_global_device_ids=true | all-gather | bytes 33024 | tf_op jit(solution)/shard_map/all_gather | solution.py:20
  60.7 1.3 dynamic-slice
  62.0 1.4 fusion.8
  63.4 0.7 compare_and_fusion
  64.1 0.7 compare_select_fusion
  64.9 7.0 gather_fusion
  71.9 3.1 add_convert_fusion
  75.0 53.0 %all-gather.3.cloned.1.call-done = bf16[1,128,32,128]{3,2,0,1:T(8,128)(2,1)} async-done(((bf16[1,1,32,128]{3,2,0,1:T(8,128)(2,1)}), bf16[1,128,32,128]{3,2,0,1:T(8,128)(2,1)}) %all-gather.3.cloned.1.call-update) | async-done | bytes 1048592 | tf_op jit(solution)/shard_map/all_gather | solution.py:19
  128.0 18.6 %while.21 = (s32[]{:T(128)}, f32[8,512]{1,0:T(8,128)S(1)}, bf16[8,512,128]{2,1,0:T(8,128)(2,1)}, bf16[4096,128]{1,0:T(8,128)(2,1)S(1)}, s32[]{:T(128)}, /*index=5*/s32[]{:T(128)}) while((s32[]{:T(128)}, f32[8,512]{1,0:T(8,128)S(1)}, bf16[8,512,128]{2,1,0:T(8,128)(2,1)}, bf16[4096,128]{1,0:T(8,128)(2,1)S(1)}, s32[]{:T(128)}, ...), condition=%wide.region_2.3_spmd, body=%wide.region_0.2_spmd.sunk | while | flops 538967552 | bytes 1185877 | solution.py:33
  128.0 2.3 convolution_reduce_fusion.2
  130.4 2.2 convolution_reduce_fusion.2
  132.7 2.2 convolution_reduce_fusion.2
  135.0 2.2 convolution_reduce_fusion.2
  137.3 2.2 convolution_reduce_fusion.2
  139.7 2.2 convolution_reduce_fusion.2
  142.0 2.2 convolution_reduce_fusion.2
  144.3 2.2 convolution_reduce_fusion.2
  146.7 488.5 %pmax.7 = f32[128,32]{1,0:T(8,128)S(1)} all-reduce(f32[128,32]{1,0:T(8,128)S(1)} %reshape.69), channel_id=1, replica_groups=mesh['shard'=128,'rep'=4] {'shard'}, use_global_device_ids=true, to_apply=%region_3.4 | all-reduce | flops 4096 | bytes 32768 | tf_op jit(solution)/shard_map/pmax | solution.py:61
  635.2 19.7 %while.22 = (s32[]{:T(128)}, f32[8,16,16]{2,1,0:T(8,128)S(1)}, bf16[8,16,32,128]{3,2,1,0:T(8,128)(2,1)}, bf16[2048,128]{1,0:T(8,128)(2,1)S(1)}, s32[16]{0:T(128)S(1)}, /*index=5*/s32[]{:T(128)}, f32[]{:T(128)}) while((s32[]{:T(128)}, f32[8,16,16]{2,1,0:T(8,128)S(1)}, bf16[8,16,32,128]{3,2,1,0:T(8,128)(2,1)}, ...), condition=%wide.region_7.8_spmd.clone, body=%wide.region_4.7_spmd.clone.sunk | while | flops 270534400 | bytes 742561 | solution.py:58
  635.3 2.2 select_reduce_fusion.3
  637.7 2.2 select_reduce_fusion.3
  640.2 2.2 select_reduce_fusion.3
  642.6 2.2 select_reduce_fusion.3
  645.1 2.2 select_reduce_fusion.3
  647.6 2.2 select_reduce_fusion.3
  650.0 2.2 select_reduce_fusion.3
  652.5 2.2 select_reduce_fusion.3
  655.2 490.9 %all-reduce = f32[128,64]{1,0:T(8,128)S(1)} all-reduce(f32[128,64]{1,0:T(8,128)S(1)} %copy.15), channel_id=2, replica_groups=mesh['shard'=128,'rep'=4] {'shard'}, use_global_device_ids=true, to_apply=%region_9.10.clone | all-reduce | flops 8192 | bytes 65536
  1146.0 0.5 dynamic-slice_bitcast_fusion.1
  1146.5 1.1 dynamic-slice_bitcast_fusion
  (50 shorter events, 2.5 us)
Async XLA Ops:
  7.2 57.7 %all-gather.5.cloned.1.call-start = ((), (), s32[]{:S(2)}) async-start(), calls=%async_computation.1 | async-start | bytes 1310720 | tf_op jit(solution)/shard_map/all_gather | solution.py:25
  7.9 120.1 %all-gather.3.cloned.1.call-start = ((), (), s32[]{:S(2)}) async-start(), calls=%async_computation | async-start | bytes 1056768 | tf_op jit(solution)/shard_map/all_gather | solution.py:19
  64.8 7.1 copy-start.1
  71.9 56.1 %copy-start = (bf16[4096,128]{1,0:T(8,128)(2,1)S(1)}, bf16[4096,128]{1,0:T(8,128)(2,1)}, u32[]{:S(2)}) copy-start(bf16[4096,128]{1,0:T(8,128)(2,1)} %all-gather.5.cloned.1.call-done) | copy-start | bytes 3145732
  128.0 507.2 %copy-start.2 = (s32[16]{0:T(128)S(1)}, s32[16]{0:T(128)}, u32[]{:S(2)}) copy-start(s32[16]{0:T(128)} %param.17) | copy-start | bytes 196
Sparse Core Ops, SparseCore 0:
  10.1 33.8 all-gather.4
  47.0 80.9 all-gather.2
where the time goes:
time: 1160 us; the launch traced here: 1150 us
  blocking collectives  1030 us (89%)
  waiting for transfers between devices  54.4 us (5%)
  matrix products  35.8 us (3%)
  between operations  14.2 us (1%)
  local copies, waits for them, and re-layouts  12.2 us (1%)
    unnamed x1, blocking collectives  491 us
    pmax x1, blocking collectives, on_device(): merged = lax.pmax(partial_best, 'shard')  488 us
    all_gather x1, waiting for transfers between devices, on_device(): lax.all_gather(queries, 'shard', axis=1, tiled=True)  53 us
    all_gather x1, blocking collectives, on_device(): lax.all_gather(candidates, 'shard', axis=1, tiled=True)  51.9 us
  transfers between devices with their start and end apart: 2, of which 1 were waited for; matrix products, arithmetic and copies ran while one was open for 1% of the time, Pallas kernels for 0%

commit v1 on v0

v1 whole, which is shorter than its diff:
```python
import functools
import math

import jax
import jax.numpy as jnp
from jax import lax
from jax.experimental import pallas as pl
from jax.experimental.pallas import tpu as pltpu

FAR_BELOW = -1e30
MESH = pl.DeviceIdType.MESH
CORES = 2
SLOTS = 8
HALF = 16
DIMS = (((1,), (1,)), ((), ()))


def kernel(
    n, nx, query_ref, cand_ref, weight_ref, length_ref, id_ref, book_hbm, code_hbm,
    best_out, score_out,
    book, book32, toks, codes, extra32, fetched, emb, best_acc, pair_best,
    cand_row, cand_line, cand_all, hits, slot_vec, slot_smem, tiles, got1, line, got2,
    local_sem, s1, r1, s2, r2, s3, r3, sc1, rc1, sc2, rc2, sc3, rc3, sb, rb, sx, rx, sy, ry,
):
    quarter = book_hbm.shape[0]
    n_pass, pass_len = id_ref.shape
    n_cand = cand_ref.shape[1]
    side = CORES * n
    n_blocks = n * side
    n_query = CORES * n * n
    width = side * HALF
    lane_half = n * HALF

    shard = lax.axis_index("shard")
    rep = lax.axis_index("rep")
    c = lax.rem(shard, CORES)
    y = lax.rem(shard // CORES, n)
    z = shard // (CORES * n)

    def at(z_, y_, c_):
        return {"shard": (z_ * n + y_) * CORES + c_, "rep": rep}

    def near(me, k, count):
        step = (k + 1) // 2
        return lax.rem(jnp.where(lax.rem(k, 2) == 1, me + step, me + count - step), count)

    def rcopy(src, dst, send, recv, dev):
        return pltpu.make_async_remote_copy(
            src_ref=src, dst_ref=dst, send_sem=send, recv_sem=recv,
            device_id=dev, device_id_type=MESH,
        )

    sibling = at(z, y, 1 - c)

    def loop(low, high, body):
        def step(k, carry):
            body(k)
            return carry
        lax.fori_loop(low, high, step, 0)

    def blocks_a(z_, c_):
        return toks.at[pl.ds((z_ * CORES + c_) * n, n)]

    def blocks_b(y_, c_):
        return toks.at[pl.ds(n_blocks + (y_ * CORES + c_) * n, n)]

    own_rows = pl.ds(pl.multiple_of(rep * quarter, quarter), quarter)
    load_book = pltpu.make_async_copy(book_hbm, book.at[own_rows], local_sem.at[0])
    load_codes = pltpu.make_async_copy(code_hbm, codes, local_sem.at[1])
    load_book.start()
    load_codes.start()

    barrier = pltpu.get_barrier_semaphore()

    def greet(dev):
        pl.semaphore_signal(barrier, inc=1, device_id=dev, device_id_type=MESH)

    def greet_line(k):
        greet(at(z, near(y, k, n), c))
        greet(at(z, near(y, k, n), 1 - c))
        greet(at(near(z, k, n), y, c))

    loop(1, n, greet_line)
    loop(1, nx, lambda k: greet({"shard": shard, "rep": near(rep, k, nx)}))
    greet(sibling)

    toks[(z * CORES + c) * n + y] = query_ref[0:HALF]
    toks[n_blocks + (y * CORES + c) * n + z] = query_ref[HALF : 2 * HALF]
    cand_row[...] = jnp.full(cand_row.shape, -1, jnp.int32)
    cand_row[:, 0:n_cand] = cand_ref[...]
    cand_line[pl.ds(y, 1)] = cand_row[...].reshape(1, 1, 128)

    pl.semaphore_wait(barrier, 3 * (n - 1) + nx)

    def hop1_copies(k):
        ty, tz = near(y, k, n), near(z, k, n)
        block_a = toks.at[(z * CORES + c) * n + y]
        block_b = toks.at[n_blocks + (y * CORES + c) * n + z]
        return (
            rcopy(cand_line.at[y], cand_line.at[y], sc1.at[k], rc1.at[y], at(z, ty, c)),
            rcopy(block_a, block_a, s1.at[0, k], r1.at[0, y], at(z, ty, c)),
            rcopy(block_b, block_b, s1.at[1, k], r1.at[1, z], at(tz, y, c)),
        )

    def book_copy(k):
        return rcopy(
            book_hbm, book.at[own_rows], sb.at[k], rb.at[rep],
            {"shard": shard, "rep": near(rep, k, nx)},
        )

    def hop1_start(k):
        for copy in hop1_copies(k):
            copy.start()

    loop(1, n, hop1_start)
    loop(1, nx, lambda k: book_copy(k).start())

    load_codes.wait()

    def residual(p):
        part = codes[p]
        value = jnp.zeros(part.shape, jnp.float32)
        for level in range(weight_ref.shape[0]):
            value = jnp.where(part == level, weight_ref[level], value)
        extra32[p] = value

    loop(0, n_pass, residual)

    def hop1_wait(k):
        ty, tz = near(y, k, n), near(z, k, n)
        block_a = toks.at[(z * CORES + c) * n + ty]
        block_b = toks.at[n_blocks + (y * CORES + c) * n + tz]
        rcopy(cand_line.at[ty], cand_line.at[ty], sc1.at[k], rc1.at[ty], sibling).wait_recv()
        rcopy(block_a, block_a, s1.at[0, k], r1.at[0, ty], sibling).wait_recv()
        rcopy(block_b, block_b, s1.at[1, k], r1.at[1, tz], sibling).wait_recv()

    loop(1, n, hop1_wait)

    def cand_slab(z_, c_):
        return cand_all.at[pl.ds(c_ * n, n), pl.ds(z_, 1)]

    def hop2_copies(k):
        ty, tz = near(y, k, n), near(z, k, n)
        return (
            rcopy(blocks_a(z, c), blocks_a(z, c), s2.at[0, k], r2.at[0, z], at(tz, y, c)),
            rcopy(blocks_b(y, c), blocks_b(y, c), s2.at[1, k], r2.at[1, y], at(z, ty, c)),
            rcopy(cand_line, cand_slab(z, c), sc2.at[k], rc2.at[z], at(tz, y, c)),
        )

    def hop2_start(k):
        for copy in hop2_copies(k):
            copy.start()

    loop(1, n, hop2_start)
    own_cands = pltpu.make_async_copy(cand_line, cand_slab(z, c), local_sem.at[2])
    own_cands.start()

    def pass_on(k, half):
        if half == 0:
            zk = near(z, k, n)
            return rcopy(blocks_a(zk, c), blocks_a(zk, c), s3.at[0, k], r3.at[0, zk], sibling)
        yk = near(y, k, n)
        return rcopy(blocks_b(yk, c), blocks_b(yk, c), s3.at[1, k], r3.at[1, yk], sibling)

    pass_on(0, 0).start()
    pass_on(0, 1).start()
    own_cands.wait()

    def tile_best(tile, first_row, fresh):
        token = toks[pl.ds(tile * side, side)].reshape(width, toks.shape[2])
        part = book[pl.ds(pl.multiple_of(first_row, quarter), quarter)]
        scored = lax.dot_general(part, token, DIMS, preferred_element_type=jnp.float32)
        top = jnp.max(scored.reshape(quarter // 8, 8, width), axis=0)
        best_acc[tile] = top if fresh else jnp.maximum(best_acc[tile], top)

    def widen(r):
        span = pl.ds(pl.multiple_of(r * quarter, quarter), quarter)
        book32[span] = book[span].astype(jnp.float32)

    load_book.wait()
    widen(rep)

    def own_pair(k):
        zk, yk = near(z, k, n), near(y, k, n)
        other_a, other_b = blocks_a(zk, 1 - c), blocks_b(yk, 1 - c)
        rcopy(other_a, other_a, s3.at[0, k], r3.at[0, zk], sibling).wait_recv()
        rcopy(other_b, other_b, s3.at[1, k], r3.at[1, yk], sibling).wait_recv()
        tile_best(zk, rep * quarter, True)
        tile_best(n + yk, rep * quarter, True)

    def arrive(k):
        zk, yk = near(z, k, n), near(y, k, n)
        rcopy(blocks_a(zk, c), blocks_a(zk, c), s2.at[0, k], r2.at[0, zk], sibling).wait_recv()
        pass_on(k, 0).start()
        rcopy(blocks_b(yk, c), blocks_b(yk, c), s2.at[1, k], r2.at[1, yk], sibling).wait_recv()
        pass_on(k, 1).start()
        own_pair(k - 1)

    loop(1, n, arrive)

    def cands_wait(k):
        zk = near(z, k, n)
        rcopy(cand_line, cand_slab(zk, c), sc2.at[k], rc2.at[zk], sibling).wait_recv()

    loop(1, n, cands_wait)

    def cand_core(c_):
        return cand_all.at[pl.ds(c_ * n, n)]

    hand_cands = rcopy(cand_core(c), cand_core(c), sc3.at[0], rc3.at[0], sibling)
    hand_cands.start()
    own_pair(n - 1)

    rcopy(cand_core(1 - c), cand_core(1 - c), sc3.at[0], rc3.at[0], sibling).wait_recv()
    cand_t = jnp.transpose(cand_all[...].reshape(n_query, 128))[0:n_cand]
    first_pass = shard * n_pass
    for p in range(n_pass):
        hits[p : p + 1, :] = jnp.max(
            jnp.where(cand_t == first_pass + p, 1.0, 0.0), axis=0, keepdims=True
        )
    hit = hits[...]
    before = (
        lax.broadcasted_iota(jnp.int32, (n_query, n_query), 0)
        < lax.broadcasted_iota(jnp.int32, (n_query, n_query), 1)
    ).astype(jnp.bfloat16)
    rank = jnp.dot(hit.astype(jnp.bfloat16), before, preferred_element_type=jnp.float32)
    rank = jnp.where(hit > 0.5, rank, -1.0)
    bits = n.bit_length() - 1
    q_index = lax.broadcasted_iota(jnp.int32, (n_pass, n_query), 1)
    q_z = q_index & (n - 1)
    q_y = (q_index >> bits) & (n - 1)
    q_c = q_index >> (2 * bits)
    at_a = ((q_z * CORES + q_c) * n + q_y).astype(jnp.float32)
    at_b = ((q_y * CORES + q_c) * n + q_z + n_blocks).astype(jnp.float32)
    lane = lax.broadcasted_iota(jnp.int32, (n_pass, 128), 1)
    slots = jnp.zeros((n_pass, 128), jnp.float32)
    for k in range(SLOTS):
        mine = rank == float(k)
        slots = jnp.where(
            lane == k, jnp.sum(jnp.where(mine, at_a, 0.0), axis=1, keepdims=True), slots
        )
        slots = jnp.where(
            lane == SLOTS + k, jnp.sum(jnp.where(mine, at_b, 0.0), axis=1, keepdims=True), slots
        )
    slot_vec[...] = slots.astype(jnp.int32)
    to_smem = pltpu.make_async_copy(slot_vec, slot_smem, local_sem.at[3])
    to_smem.start()

    def other_quarter(k):
        r = near(rep, k, nx)
        span = pl.ds(pl.multiple_of(r * quarter, quarter), quarter)
        rcopy(book_hbm, book.at[span], sb.at[k], rb.at[r], sibling).wait_recv()
        widen(r)

        def half(h):
            for t in range(n):
                tile_best(h * n + t, r * quarter, False)

        loop(0, 2, half)

    loop(1, nx, other_quarter)
    to_smem.wait()

    group = 32

    def fetch(i):
        p = i // (pass_len // group)
        s0 = lax.rem(i, pass_len // group) * group
        for u in range(group):
            row = id_ref[p, s0 + u]
            fetched[pl.ds(i * group + u, 1)] = book32[pl.ds(row, 1)]

    loop(0, n_pass * pass_len // group, fetch)

    def decode(p):
        span = pl.ds(pl.multiple_of(p * pass_len, pass_len), pass_len)
        emb[span] = (fetched[span] + extra32[p]).astype(jnp.bfloat16)

    loop(0, n_pass, decode)

    slot_iota = lax.broadcasted_iota(jnp.int32, (pass_len, SLOTS * 2 * HALF), 0)

    def score(i):
        for u in range(4):
            p = i * 4 + u
            parts = []
            for k in range(SLOTS):
                parts.append(toks[jnp.clip(slot_smem[p, k], 0, n_blocks - 1)])
                parts.append(
                    toks[jnp.clip(slot_smem[p, SLOTS + k], n_blocks, 2 * n_blocks - 1)]
                )
            picked = jnp.concatenate(parts, axis=0)
            span = pl.ds(pl.multiple_of(p * pass_len, pass_len), pass_len)
            similar = lax.dot_general(
                emb[span], picked, DIMS, preferred_element_type=jnp.float32
            )
            similar = jnp.where(slot_iota < length_ref[p], similar, FAR_BELOW)
            pair_best[pl.ds(p, 1)] = jnp.max(similar, axis=0, keepdims=True)

    loop(0, n_pass // 4, score)

    tok_of = lax.broadcasted_iota(jnp.int32, (SLOTS * 2 * HALF, 128), 0) >> 5
    col_of = lax.broadcasted_iota(jnp.int32, (SLOTS * 2 * HALF, 128), 1)
    ones = (tok_of == col_of).astype(jnp.float32)
    slot_score = jnp.dot(
        pair_best[...], ones, preferred_element_type=jnp.float32,
        precision=lax.Precision.HIGHEST,
    )
    table = jnp.zeros((n_pass, n_query), jnp.float32)
    for k in range(SLOTS):
        table = jnp.where(rank == float(k), slot_score[:, k : k + 1], table)
    chosen = jnp.full((n_cand, n_query), FAR_BELOW, jnp.float32)
    for p in range(n_pass):
        chosen = jnp.where(cand_t == first_pass + p, table[p : p + 1, :], chosen)
    chosen = jnp.transpose(
        jnp.concatenate([chosen, jnp.full((128 - n_cand, n_query), FAR_BELOW, jnp.float32)], axis=0)
    )

    best = jnp.max(best_acc[...], axis=1)
    row_of = lax.broadcasted_iota(jnp.int32, (n, 128), 0)
    lane_of = lax.broadcasted_iota(jnp.int32, (n, 128), 1)
    in_a = (lane_of >= n_cand) & (lane_of < n_cand + HALF)
    in_b = (lane_of >= n_cand + HALF) & (lane_of < n_cand + 2 * HALF)

    def fit(part):
        if lane_half == 128:
            return part
        return jnp.concatenate([part, jnp.full((n, 128 - lane_half), FAR_BELOW, jnp.float32)], axis=1)

    for c_ in range(CORES):
        cols = slice(c_ * lane_half, (c_ + 1) * lane_half)
        best_a = fit(best[0:n, cols])
        best_b = fit(best[n : 2 * n, cols])
        for y_ in range(n):
            shift = (n_cand - y_ * HALF) % 128
            part_a = pltpu.roll(best_a, shift, 1) if shift else best_a
            part_b = jnp.where(
                (lane_of >> 4) == row_of, jnp.broadcast_to(best_b[y_ : y_ + 1], (n, 128)), FAR_BELOW
            )
            for step in (64, 32, 16):
                part_b = jnp.maximum(part_b, pltpu.roll(part_b, step, 1))
            t = c_ * n + y_
            tile = chosen[t * n : (t + 1) * n]
            tiles[t] = jnp.where(in_a, part_a, jnp.where(in_b, part_b, tile))

    me = c * n + y

    def merge1_copy(k, c_):
        ty = near(y, k, n)
        return rcopy(
            tiles.at[c_ * n + ty], got1.at[me], sx.at[c_ * n + ty], rx.at[me], at(z, ty, c_)
        )

    def merge1_start(k):
        merge1_copy(k, c).start()
        merge1_copy(k, 1 - c).start()

    loop(1, n, merge1_start)
    merge1_copy(0, 1 - c).start()

    def from1(k, c_):
        t = c_ * n + near(y, k, n)
        rcopy(tiles.at[t], got1.at[t], sx.at[t], rx.at[t], sibling).wait_recv()
        return got1[t]

    merged = lax.fori_loop(
        1, n,
        lambda k, acc: jnp.maximum(acc, jnp.maximum(from1(k, c), from1(k, 1 - c))),
        tiles[me],
    )
    merged = jnp.maximum(merged, from1(0, 1 - c))
    line[...] = merged

    def merge2_copy(k):
        tz = near(z, k, n)
        return rcopy(line.at[pl.ds(tz, 1)], got2.at[pl.ds(z, 1)], sy.at[k], ry.at[z], at(tz, y, c))

    loop(1, n, lambda k: merge2_copy(k).start())

    def from2(k, acc):
        tz = near(z, k, n)
        row = got2.at[pl.ds(tz, 1)]
        rcopy(row, row, sy.at[k], ry.at[tz], sibling).wait_recv()
        return jnp.maximum(acc, got2[pl.ds(tz, 1)])

    final = lax.fori_loop(1, n, from2, line[pl.ds(z, 1)])
    score_out[...] = final[:, 0:n_cand]
    best_out[...] = pltpu.roll(final, 128 - n_cand, 1)[:, 0 : 2 * HALF]

    def sent(k):
        for copy in hop1_copies(k) + hop2_copies(k):
            copy.wait_send()
        pass_on(k, 0).wait_send()
        pass_on(k, 1).wait_send()
        merge1_copy(k, c).wait_send()
        merge1_copy(k, 1 - c).wait_send()
        merge2_copy(k).wait_send()

    loop(1, n, sent)
    loop(1, nx, lambda k: book_copy(k).wait_send())
    pass_on(0, 0).wait_send()
    pass_on(0, 1).wait_send()
    hand_cands.wait_send()
    merge1_copy(0, 1 - c).wait_send()


def on_device(
    queries, candidates, codebook, bucket_weights, centroid_ids, residual_codes, passage_lengths, sizes
):
    n, nx = sizes
    query_len, width = queries.shape[2:]
    n_cand = candidates.shape[2]
    quarter = codebook.shape[0]
    n_pass, pass_len = centroid_ids.shape
    n_query = CORES * n * n
    tile_width = CORES * n * HALF
    vmem = pl.BlockSpec(memory_space=pltpu.VMEM)
    smem = pl.BlockSpec(memory_space=pltpu.SMEM)
    hbm = pl.BlockSpec(memory_space=pl.ANY)
    dma = pltpu.SemaphoreType.DMA
    f32, bf16, i32 = jnp.float32, jnp.bfloat16, jnp.int32
    best, scores = pl.pallas_call(
        functools.partial(kernel, n, nx),
        out_shape=(
            jax.ShapeDtypeStruct((1, query_len), f32),
            jax.ShapeDtypeStruct((1, n_cand), f32),
        ),
        in_specs=[vmem, vmem, smem, smem, smem, hbm, hbm],
        out_specs=(vmem, vmem),
        scratch_shapes=[
            pltpu.VMEM((nx * quarter, width), bf16),
            pltpu.VMEM((nx * quarter, width), f32),
            pltpu.VMEM((2 * n_query, HALF, width), bf16),
            pltpu.VMEM(residual_codes.shape, i32),
            pltpu.VMEM(residual_codes.shape, f32),
            pltpu.VMEM((n_pass * pass_len, width), f32),
            pltpu.VMEM((n_pass * pass_len, width), bf16),
            pltpu.VMEM((2 * n, 8, tile_width), f32),
            pltpu.VMEM((n_pass, SLOTS * 2 * HALF), f32),
            pltpu.VMEM((1, 128), i32),
            pltpu.VMEM((n, 1, 128), i32),
            pltpu.VMEM((CORES * n, n, 128), i32),
            pltpu.VMEM((n_pass, n_query), f32),
            pltpu.VMEM((n_pass, 128), i32),
            pltpu.SMEM((n_pass, 128), i32),
            pltpu.VMEM((CORES * n, n, 128), f32),
            pltpu.VMEM((CORES * n, n, 128), f32),
            pltpu.VMEM((n, 128), f32),
            pltpu.VMEM((n, 128), f32),
            dma((4,)),
            dma((2, n)), dma((2, n)),
            dma((2, n)), dma((2, n)),
            dma((2, n)), dma((2, n)),
            dma((n,)), dma((n,)),
            dma((n,)), dma((n,)),
            dma((1,)), dma((1,)),
            dma((nx,)), dma((nx,)),
            dma((CORES * n,)), dma((CORES * n,)),
            dma((n,)), dma((n,)),
        ],
        compiler_params=pltpu.CompilerParams(
            collective_id=0, has_side_effects=True, vmem_limit_bytes=40 << 20
        ),
        cost_estimate=pl.CostEstimate(flops=4 << 30, bytes_accessed=2 << 20, transcendentals=0),
        name="late_interaction",
    )(
        queries.reshape(query_len, width), candidates.reshape(1, n_cand), bucket_weights,
        passage_lengths, centroid_ids, codebook, residual_codes,
    )
    return best.reshape(1, 1, query_len), scores.reshape(1, 1, n_cand)


def solution(mesh):
    from jax.sharding import PartitionSpec as P

    nx = mesh.shape["rep"]
    n = math.isqrt(mesh.shape["shard"] // CORES)
    in_specs = (
        P("rep", "shard", None, None),
        P("rep", "shard", None),
        P(("shard", "rep"), None),
        P(),
        P("shard", None),
        P("shard", None, None),
        P("shard"),
    )
    out_specs = (P("rep", "shard", None), P("rep", "shard", None))
    return jax.shard_map(
        functools.partial(on_device, sizes=(n, nx)),
        mesh=mesh, in_specs=in_specs, out_specs=out_specs, check_vma=False,
    )
```

time: 1160 us -> 63.5 us (0.05)
  blocking collectives: 1030 us -> 0 us
  Pallas kernels: 0 us -> 57.2 us
  waiting for transfers between devices: 54.4 us -> 0 us
  matrix products: 35.8 us -> 0 us
  between operations: 14.2 us -> 0.67 us
    unnamed x1 -> x0, blocking collectives: 491 us -> none
    pmax x1 -> x0, blocking collectives: 488 us -> none  [on_device(): merged = lax.pmax(partial_best, 'shard')]
    pallas_call x0 -> x1, Pallas kernels: none -> 57.2 us  [on_device(): pl.pallas_call(functools.partial(kernel, n, nx), out_shape=(jax.ShapeDtyp...]
    all_gather x2 -> x0, waiting for transfers between devices: 53 us -> none  [the longest x1 53 us: on_device(): lax.all_gather(queries, 'shard', axis=1, tiled=True)]
    all_gather x1 -> x0, blocking collectives: 51.9 us -> none  [on_device(): lax.all_gather(candidates, 'shard', axis=1, tiled=True)]
    dot_general x16 -> x0, matrix products: 35.8 us -> none  [the longest x8 18 us: best_block(): jnp.dot(row_block, shard_book.T, preferred_element_type=jnp.float32)]
  transfers between devices with their start and end apart: 2 -> 0, of which waited for: 1 -> 0; matrix products, arithmetic and copies ran while one was open for 1% -> 0% of each run, Pallas kernels for 0% -> 0%
where the time goes in v1:
time: 63.5 us; the launch traced here: 63.1 us
  Pallas kernels  57.2 us (90%)
  local copies, waits for them, and re-layouts  5.25 us (8%)
  between operations  0.67 us (1%)
    pallas_call x1, Pallas kernels, on_device(): pl.pallas_call(functools.partial(kernel, n, nx), out_shape=(jax.ShapeDtyp...  57.2 us
    unnamed x16, local copies, waits for them, and re-layouts  5.25 us

profile of v1, /device:TPU:1, one launch (start us, length us, event | category | flops | bytes accessed | tf_op | source)
XLA Modules:
  0.0 63.1 jit_solution(2800502803029263208)
XLA Ops:
  0.6 0.0 copy-start.4
  0.6 0.0 copy-start.5
  0.7 0.0 copy-start.6
  0.7 0.6 copy-done.4
  1.3 0.0 copy-done.5
  1.3 0.0 copy-done.6
  1.3 0.0 copy-start
  1.3 1.2 %copy-done = s32[16,128,128]{2,1,0:T(8,128)S(1)} copy-done((s32[16,128,128]{2,1,0:T(8,128)S(1)}, s32[16,128,128]{2,1,0:T(8,128)}, u32[]{:S(2)}) %copy-start) | copy-done | bytes 1048600
  2.5 0.0 copy-start.1
  2.5 0.9 %copy-done.1 = bf16[1024,128]{1,0:T(8,128)(2,1)S(1)} copy-done((bf16[1024,128]{1,0:T(8,128)(2,1)S(1)}, bf16[1024,128]{1,0:T(8,128)(2,1)}, u32[]{:S(2)}) %copy-start.1) | copy-done | bytes 262168
  3.5 0.0 copy-start.2
  3.5 0.7 %copy-done.2 = bf16[1,1,32,128]{3,2,1,0:T(8,128)(2,1)S(1)} copy-done((bf16[1,1,32,128]{3,2,1,0:T(8,128)(2,1)S(1)}, bf16[1,1,32,128]{3,2,1,0:T(8,128)(2,1)}, u32[]{:S(2)}) %copy-start.2) | copy-done | bytes 8216
  4.2 0.0 copy-start.3
  4.2 0.7 %copy-done.3 = s32[16,128]{1,0:T(8,128)S(1)} copy-done((s32[16,128]{1,0:T(8,128)S(1)}, s32[16,128]{1,0:T(8,128)}, u32[]{:S(2)}) %copy-start.3) | copy-done | bytes 8216
  4.9 57.2 %late_interaction.1 = (f32[1,32]{1,0:T(1,128)S(1)}, f32[1,64]{1,0:T(1,128)S(1)}) custom-call(bf16[32,128]{1,0:T(8,128)(2,1)S(1)} %bitcast.4, s32[1,64]{1,0:T(1,128)S(1)} %bitcast.5, f32[4]{0:T(128)S(1)} %copy-done.5, s32[16]{0:T(128)S(1)} %copy-done.6, s32[16,128]{1,0:T(8,128)S(1)} %copy-done.3, bf16[1024,128]{1,0:T(8,128)(2,1)S(1)} %copy-done.1, ...), custom_call_target="tpu_custom_call" | custom-call | flops 4294967296 | bytes 2097152 | tf_op jit(solution)/shard_map/late_interaction/pallas_call | solution.py:422
  62.0 0.5 copy.11
  62.6 0.5 copy.12
Async XLA Ops:
  0.6 0.7 %copy-start.4 = (s32[1,1,64]{2,1,0:T(1,128)S(1)}, s32[1,1,64]{2,1,0:T(1,128)}, u32[]{:S(2)}) copy-start(s32[1,1,64]{2,1,0:T(1,128)} %param.8) | copy-start | bytes 772
  0.6 0.7 %copy-start.5 = (f32[4]{0:T(128)S(1)}, f32[4]{0:T(128)}, u32[]{:S(2)}) copy-start(f32[4]{0:T(128)} %weight_ref.1) | copy-start | bytes 52
  0.7 0.7 %copy-start.6 = (s32[16]{0:T(128)S(1)}, s32[16]{0:T(128)}, u32[]{:S(2)}) copy-start(s32[16]{0:T(128)} %length_ref.1) | copy-start | bytes 196
  1.3 1.2 %copy-start = (s32[16,128,128]{2,1,0:T(8,128)S(1)}, s32[16,128,128]{2,1,0:T(8,128)}, u32[]{:S(2)}) copy-start(s32[16,128,128]{2,1,0:T(8,128)} %code_hbm.1) | copy-start | bytes 3145732
  2.5 0.9 %copy-start.1 = (bf16[1024,128]{1,0:T(8,128)(2,1)S(1)}, bf16[1024,128]{1,0:T(8,128)(2,1)}, u32[]{:S(2)}) copy-start(bf16[1024,128]{1,0:T(8,128)(2,1)} %book_hbm.1) | copy-start | bytes 786436
  3.5 0.7 %copy-start.2 = (bf16[1,1,32,128]{3,2,1,0:T(8,128)(2,1)S(1)}, bf16[1,1,32,128]{3,2,1,0:T(8,128)(2,1)}, u32[]{:S(2)}) copy-start(bf16[1,1,32,128]{3,2,1,0:T(8,128)(2,1)} %param.7) | copy-start | bytes 24580
  4.2 0.7 %copy-start.3 = (s32[16,128]{1,0:T(8,128)S(1)}, s32[16,128]{1,0:T(8,128)}, u32[]{:S(2)}) copy-start(s32[16,128]{1,0:T(8,128)} %id_ref.1) | copy-start | bytes 24580

commit v2 on v1

--- a/solution.py
+++ b/solution.py
@@ -16,8 +16,9 @@
 
 
 def kernel(
-    n, nx, query_ref, cand_ref, weight_ref, length_ref, id_ref, book_hbm, code_hbm,
+    n, nx, query_hbm, cand_hbm, weight_hbm, length_hbm, id_hbm, book_hbm, code_hbm,
     best_out, score_out,
+    query_ref, cand_ref, weight_ref, length_ref, id_ref,
     book, book32, toks, codes, extra32, fetched, emb, best_acc, pair_best,
     cand_row, cand_line, cand_all, hits, slot_vec, slot_smem, tiles, got1, line, got2,
     local_sem, s1, r1, s2, r2, s3, r3, sc1, rc1, sc2, rc2, sc3, rc3, sb, rb, sx, rx, sy, ry,
@@ -67,6 +68,15 @@
     own_rows = pl.ds(pl.multiple_of(rep * quarter, quarter), quarter)
     load_book = pltpu.make_async_copy(book_hbm, book.at[own_rows], local_sem.at[0])
     load_codes = pltpu.make_async_copy(code_hbm, codes, local_sem.at[1])
+    small = [
+        pltpu.make_async_copy(source, target, local_sem.at[4 + i])
+        for i, (source, target) in enumerate((
+            (query_hbm, query_ref), (cand_hbm, cand_ref), (weight_hbm, weight_ref),
+            (length_hbm, length_ref), (id_hbm, id_ref),
+        ))
+    ]
+    for copy in small:
+        copy.start()
     load_book.start()
     load_codes.start()
 
@@ -84,6 +94,8 @@
     loop(1, nx, lambda k: greet({"shard": shard, "rep": near(rep, k, nx)}))
     greet(sibling)
 
+    for copy in small:
+        copy.wait()
     toks[(z * CORES + c) * n + y] = query_ref[0:HALF]
     toks[n_blocks + (y * CORES + c) * n + z] = query_ref[HALF : 2 * HALF]
     cand_row[...] = jnp.full(cand_row.shape, -1, jnp.int32)
@@ -166,37 +178,51 @@
     pass_on(0, 1).start()
     own_cands.wait()
 
-    def tile_best(tile, first_row, fresh):
+    def span_of(r):
+        return pl.ds(pl.multiple_of(r * quarter, quarter), quarter)
+
+    def best_of(tile, r):
         token = toks[pl.ds(tile * side, side)].reshape(width, toks.shape[2])
-        part = book[pl.ds(pl.multiple_of(first_row, quarter), quarter)]
-        scored = lax.dot_general(part, token, DIMS, preferred_element_type=jnp.float32)
-        top = jnp.max(scored.reshape(quarter // 8, 8, width), axis=0)
-        best_acc[tile] = top if fresh else jnp.maximum(best_acc[tile], top)
+        scored = lax.dot_general(book[span_of(r)], token, DIMS, preferred_element_type=jnp.float32)
+        return jnp.max(scored.reshape(quarter // 8, 8, width), axis=0)
 
     def widen(r):
-        span = pl.ds(pl.multiple_of(r * quarter, quarter), quarter)
-        book32[span] = book[span].astype(jnp.float32)
-
-    load_book.wait()
-    widen(rep)
-
-    def own_pair(k):
+        book32[span_of(r)] = book[span_of(r)].astype(jnp.float32)
+
+    def take_quarter(k):
+        r = near(rep, k, nx)
+        span = book.at[span_of(r)]
+        rcopy(book_hbm, span, sb.at[k], rb.at[r], sibling).wait_recv()
+        widen(r)
+
+    def pair(k):
         zk, yk = near(z, k, n), near(y, k, n)
         other_a, other_b = blocks_a(zk, 1 - c), blocks_b(yk, 1 - c)
         rcopy(other_a, other_a, s3.at[0, k], r3.at[0, zk], sibling).wait_recv()
         rcopy(other_b, other_b, s3.at[1, k], r3.at[1, yk], sibling).wait_recv()
-        tile_best(zk, rep * quarter, True)
-        tile_best(n + yk, rep * quarter, True)
-
-    def arrive(k):
+        for tile in (zk, n + yk):
+            top = best_of(tile, rep)
+            for j in range(1, nx - 1):
+                top = jnp.maximum(top, best_of(tile, near(rep, j, nx)))
+            best_acc[tile] = top
+
+    def forward(k):
         zk, yk = near(z, k, n), near(y, k, n)
         rcopy(blocks_a(zk, c), blocks_a(zk, c), s2.at[0, k], r2.at[0, zk], sibling).wait_recv()
         pass_on(k, 0).start()
         rcopy(blocks_b(yk, c), blocks_b(yk, c), s2.at[1, k], r2.at[1, yk], sibling).wait_recv()
         pass_on(k, 1).start()
-        own_pair(k - 1)
-
-    loop(1, n, arrive)
+
+    load_book.wait()
+    widen(rep)
+    forward(1)
+    loop(1, nx - 1, take_quarter)
+
+    def arrive(k):
+        forward(k)
+        pair(k - 2)
+
+    loop(2, n, arrive)
 
     def cands_wait(k):
         zk = near(z, k, n)
@@ -209,7 +235,7 @@
 
     hand_cands = rcopy(cand_core(c), cand_core(c), sc3.at[0], rc3.at[0], sibling)
     hand_cands.start()
-    own_pair(n - 1)
+    loop(n - 2, n, pair)
 
     rcopy(cand_core(1 - c), cand_core(1 - c), sc3.at[0], rc3.at[0], sibling).wait_recv()
     cand_t = jnp.transpose(cand_all[...].reshape(n_query, 128))[0:n_cand]
@@ -246,37 +272,28 @@
     to_smem = pltpu.make_async_copy(slot_vec, slot_smem, local_sem.at[3])
     to_smem.start()
 
-    def other_quarter(k):
-        r = near(rep, k, nx)
-        span = pl.ds(pl.multiple_of(r * quarter, quarter), quarter)
-        rcopy(book_hbm, book.at[span], sb.at[k], rb.at[r], sibling).wait_recv()
-        widen(r)
-
-        def half(h):
-            for t in range(n):
-                tile_best(h * n + t, r * quarter, False)
-
-        loop(0, 2, half)
-
-    loop(1, nx, other_quarter)
-    to_smem.wait()
-
-    group = 32
-
-    def fetch(i):
-        p = i // (pass_len // group)
-        s0 = lax.rem(i, pass_len // group) * group
-        for u in range(group):
-            row = id_ref[p, s0 + u]
-            fetched[pl.ds(i * group + u, 1)] = book32[pl.ds(row, 1)]
-
-    loop(0, n_pass * pass_len // group, fetch)
+    take_quarter(nx - 1)
+
+    def fetch(p):
+        for u in range(pass_len):
+            fetched[pl.ds(p * pass_len + u, 1)] = book32[pl.ds(id_ref[p, u], 1)]
+
+    loop(0, n_pass, fetch)
 
     def decode(p):
         span = pl.ds(pl.multiple_of(p * pass_len, pass_len), pass_len)
         emb[span] = (fetched[span] + extra32[p]).astype(jnp.bfloat16)
 
     loop(0, n_pass, decode)
+
+    def last_quarter(h):
+        r = near(rep, nx - 1, nx)
+        for t in range(n):
+            tile = h * n + t
+            best_acc[tile] = jnp.maximum(best_acc[tile], best_of(tile, r))
+
+    loop(0, 2, last_quarter)
+    to_smem.wait()
 
     slot_iota = lax.broadcasted_iota(jnp.int32, (pass_len, SLOTS * 2 * HALF), 0)
 
@@ -415,8 +432,7 @@
     n_query = CORES * n * n
     tile_width = CORES * n * HALF
     vmem = pl.BlockSpec(memory_space=pltpu.VMEM)
-    smem = pl.BlockSpec(memory_space=pltpu.SMEM)
-    hbm = pl.BlockSpec(memory_space=pl.ANY)
+    hbm = pl.BlockSpec(memory_space=pltpu.HBM)
     dma = pltpu.SemaphoreType.DMA
     f32, bf16, i32 = jnp.float32, jnp.bfloat16, jnp.int32
     best, scores = pl.pallas_call(
@@ -425,9 +441,14 @@
             jax.ShapeDtypeStruct((1, query_len), f32),
             jax.ShapeDtypeStruct((1, n_cand), f32),
         ),
-        in_specs=[vmem, vmem, smem, smem, smem, hbm, hbm],
+        in_specs=[hbm] * 7,
         out_specs=(vmem, vmem),
         scratch_shapes=[
+            pltpu.VMEM((query_len, width), bf16),
+            pltpu.VMEM((1, n_cand), i32),
+            pltpu.SMEM(bucket_weights.shape, f32),
+            pltpu.SMEM(passage_lengths.shape, i32),
+            pltpu.SMEM(centroid_ids.shape, i32),
             pltpu.VMEM((nx * quarter, width), bf16),
             pltpu.VMEM((nx * quarter, width), f32),
             pltpu.VMEM((2 * n_query, HALF, width), bf16),
@@ -447,7 +468,7 @@
             pltpu.VMEM((CORES * n, n, 128), f32),
             pltpu.VMEM((n, 128), f32),
             pltpu.VMEM((n, 128), f32),
-            dma((4,)),
+            dma((9,)),
             dma((2, n)), dma((2, n)),
             dma((2, n)), dma((2, n)),
             dma((2, n)), dma((2, n)),
@@ -459,7 +480,7 @@
             dma((n,)), dma((n,)),
         ],
         compiler_params=pltpu.CompilerParams(
-            collective_id=0, has_side_effects=True, vmem_limit_bytes=40 << 20
+            collective_id=0, has_side_effects=True, vmem_limit_bytes=60 << 20
         ),
         cost_estimate=pl.CostEstimate(flops=4 << 30, bytes_accessed=2 << 20, transcendentals=0),
         name="late_interaction",

time: 63.5 us -> 53.6 us (0.84)
  Pallas kernels: 57.2 us -> 51 us
  local copies, waits for them, and re-layouts: 5.25 us -> 1.8 us
    pallas_call x1, Pallas kernels: 57.2 us -> 51 us  [on_device(): pl.pallas_call(functools.partial(kernel, n, nx), out_shape=(jax.ShapeDtyp...]
    unnamed x16 -> x6, local copies, waits for them, and re-layouts: 5.25 us -> 1.8 us
where the time goes in v2:
time: 53.6 us; the launch traced here: 53.4 us
  Pallas kernels  51 us (95%)
  local copies, waits for them, and re-layouts  1.8 us (3%)
  between operations  0.65 us (1%)
    pallas_call x1, Pallas kernels, on_device(): pl.pallas_call(functools.partial(kernel, n, nx), out_shape=(jax.ShapeDtyp...  51 us
    unnamed x6, local copies, waits for them, and re-layouts  1.8 us

profile of v2, /device:TPU:1, one launch (start us, length us, event | category | flops | bytes accessed | tf_op | source)
XLA Modules:
  0.0 53.4 jit_solution(11199373943511198650)
XLA Ops:
  0.6 51.0 %late_interaction.1 = (f32[1,32]{1,0:T(1,128)}, f32[1,64]{1,0:T(1,128)}) custom-call(bf16[32,128]{1,0:T(8,128)(2,1)} %bitcast.4, s32[1,64]{1,0:T(1,128)} %bitcast.5, f32[4]{0:T(128)} %weight_hbm.1, s32[16]{0:T(128)} %length_hbm.1, s32[16,128]{1,0:T(8,128)} %id_hbm.1, bf16[1024,128]{1,0:T(8,128)(2,1)} %book_hbm.1, s32[16,128,128]{2,1,0:T(8,128)} %code_hbm.1), custom_call_target="tpu_custom_call" | custom-call | flops 4294967296 | bytes 2097152 | tf_op jit(solution)/shard_map/late_interaction/pallas_call | solution.py:438
  51.6 0.0 copy-start.1
  51.6 0.7 %copy-done.1 = f32[1,32]{1,0:T(1,128)S(1)} copy-done((f32[1,32]{1,0:T(1,128)S(1)}, f32[1,32]{1,0:T(1,128)}, u32[]{:S(2)}) %copy-start.1) | copy-done | bytes 152
  52.3 0.0 copy-start
  52.3 0.5 copy.11
  52.8 0.1 copy-done
  52.9 0.5 copy.12
Async XLA Ops:
  51.6 0.7 %copy-start.1 = (f32[1,32]{1,0:T(1,128)S(1)}, f32[1,32]{1,0:T(1,128)}, u32[]{:S(2)}) copy-start(f32[1,32]{1,0:T(1,128)} %get-tuple-element.4) | copy-start | bytes 388
  52.3 0.6 %copy-start = (f32[1,64]{1,0:T(1,128)S(1)}, f32[1,64]{1,0:T(1,128)}, u32[]{:S(2)}) copy-start(f32[1,64]{1,0:T(1,128)} %get-tuple-element.5) | copy-start | bytes 772

commit v3 on v2

--- a/solution.py
+++ b/solution.py
@@ -17,7 +17,7 @@
 
 def kernel(
     n, nx, query_hbm, cand_hbm, weight_hbm, length_hbm, id_hbm, book_hbm, code_hbm,
-    best_out, score_out,
+    row_out,
     query_ref, cand_ref, weight_ref, length_ref, id_ref,
     book, book32, toks, codes, extra32, fetched, emb, best_acc, pair_best,
     cand_row, cand_line, cand_all, hits, slot_vec, slot_smem, tiles, got1, line, got2,
@@ -215,14 +215,18 @@
 
     load_book.wait()
     widen(rep)
+    loop(1, nx - 1, take_quarter)
+    pair(0)
     forward(1)
-    loop(1, nx - 1, take_quarter)
+
+    if n > 2:
+        forward(2)
 
     def arrive(k):
         forward(k)
         pair(k - 2)
 
-    loop(2, n, arrive)
+    loop(3, n, arrive)
 
     def cands_wait(k):
         zk = near(z, k, n)
@@ -235,7 +239,7 @@
 
     hand_cands = rcopy(cand_core(c), cand_core(c), sc3.at[0], rc3.at[0], sibling)
     hand_cands.start()
-    loop(n - 2, n, pair)
+    loop(max(1, n - 2), n, pair)
 
     rcopy(cand_core(1 - c), cand_core(1 - c), sc3.at[0], rc3.at[0], sibling).wait_recv()
     cand_t = jnp.transpose(cand_all[...].reshape(n_query, 128))[0:n_cand]
@@ -375,6 +379,18 @@
     loop(1, n, merge1_start)
     merge1_copy(0, 1 - c).start()
 
+    def gathered(k):
+        for copy in hop1_copies(k) + hop2_copies(k):
+            copy.wait_send()
+        pass_on(k, 0).wait_send()
+        pass_on(k, 1).wait_send()
+
+    loop(1, n, gathered)
+    loop(1, nx, lambda k: book_copy(k).wait_send())
+    pass_on(0, 0).wait_send()
+    pass_on(0, 1).wait_send()
+    hand_cands.wait_send()
+
     def from1(k, c_):
         t = c_ * n + near(y, k, n)
         rcopy(tiles.at[t], got1.at[t], sx.at[t], rx.at[t], sibling).wait_recv()
@@ -394,6 +410,13 @@
 
     loop(1, n, lambda k: merge2_copy(k).start())
 
+    def merge1_sent(k):
+        merge1_copy(k, c).wait_send()
+        merge1_copy(k, 1 - c).wait_send()
+
+    loop(1, n, merge1_sent)
+    merge1_copy(0, 1 - c).wait_send()
+
     def from2(k, acc):
         tz = near(z, k, n)
         row = got2.at[pl.ds(tz, 1)]
@@ -401,24 +424,8 @@
         return jnp.maximum(acc, got2[pl.ds(tz, 1)])
 
     final = lax.fori_loop(1, n, from2, line[pl.ds(z, 1)])
-    score_out[...] = final[:, 0:n_cand]
-    best_out[...] = pltpu.roll(final, 128 - n_cand, 1)[:, 0 : 2 * HALF]
-
-    def sent(k):
-        for copy in hop1_copies(k) + hop2_copies(k):
-            copy.wait_send()
-        pass_on(k, 0).wait_send()
-        pass_on(k, 1).wait_send()
-        merge1_copy(k, c).wait_send()
-        merge1_copy(k, 1 - c).wait_send()
-        merge2_copy(k).wait_send()
-
-    loop(1, n, sent)
-    loop(1, nx, lambda k: book_copy(k).wait_send())
-    pass_on(0, 0).wait_send()
-    pass_on(0, 1).wait_send()
-    hand_cands.wait_send()
-    merge1_copy(0, 1 - c).wait_send()
+    row_out[...] = final
+    loop(1, n, lambda k: merge2_copy(k).wait_send())
 
 
 def on_device(
@@ -435,14 +442,11 @@
     hbm = pl.BlockSpec(memory_space=pltpu.HBM)
     dma = pltpu.SemaphoreType.DMA
     f32, bf16, i32 = jnp.float32, jnp.bfloat16, jnp.int32
-    best, scores = pl.pallas_call(
+    row = pl.pallas_call(
         functools.partial(kernel, n, nx),
-        out_shape=(
-            jax.ShapeDtypeStruct((1, query_len), f32),
-            jax.ShapeDtypeStruct((1, n_cand), f32),
-        ),
+        out_shape=jax.ShapeDtypeStruct((1, 128), f32),
         in_specs=[hbm] * 7,
-        out_specs=(vmem, vmem),
+        out_specs=vmem,
         scratch_shapes=[
             pltpu.VMEM((query_len, width), bf16),
             pltpu.VMEM((1, n_cand), i32),
@@ -488,7 +492,8 @@
         queries.reshape(query_len, width), candidates.reshape(1, n_cand), bucket_weights,
         passage_lengths, centroid_ids, codebook, residual_codes,
     )
-    return best.reshape(1, 1, query_len), scores.reshape(1, 1, n_cand)
+    row = row.reshape(1, 1, 128)
+    return row[:, :, n_cand : n_cand + query_len], row[:, :, 0:n_cand]
 
 
 def solution(mesh):

time: 53.6 us -> 53.3 us (level)
    unnamed x6 -> x3, local copies, waits for them, and re-layouts: 1.8 us -> 1.1 us
    slice x0 -> x1, local copies, waits for them, and re-layouts: none -> 0.58 us  [on_device(): return (row[:, :, n_cand:n_cand + query_len], row[:, :, 0:n_cand])]
where the time goes in v3:
time: 53.3 us; the launch traced here: 53.1 us
  Pallas kernels  50.8 us (95%)
  local copies, waits for them, and re-layouts  1.68 us (3%)
  between operations  0.65 us (1%)
    pallas_call x1, Pallas kernels, on_device(): pl.pallas_call(functools.partial(kernel, n, nx), out_shape=jax.ShapeDtype...  50.8 us
    unnamed x3, local copies, waits for them, and re-layouts  1.1 us

profile of v3, /device:TPU:1, one launch (start us, length us, event | category | flops | bytes accessed | tf_op | source)
XLA Modules:
  0.0 53.1 jit_solution(18313783625159473641)
XLA Ops:
  0.6 50.8 %late_interaction.1 = f32[1,128]{1,0:T(1,128)} custom-call(bf16[32,128]{1,0:T(8,128)(2,1)} %bitcast.4, s32[1,64]{1,0:T(1,128)} %bitcast.5, f32[4]{0:T(128)} %weight_hbm.1, s32[16]{0:T(128)} %length_hbm.1, s32[16,128]{1,0:T(8,128)} %id_hbm.1, bf16[1024,128]{1,0:T(8,128)(2,1)} %book_hbm.1, s32[16,128,128]{2,1,0:T(8,128)} %code_hbm.1), custom_call_target="tpu_custom_call" | custom-call | flops 4294967296 | bytes 2097152 | tf_op jit(solution)/shard_map/late_interaction/pallas_call | solution.py:445
  51.4 0.0 copy-start
  51.4 0.6 %copy-done = f32[1,128]{1,0:T(1,128)S(1)} copy-done((f32[1,128]{1,0:T(1,128)S(1)}, f32[1,128]{1,0:T(1,128)}, u32[]{:S(2)}) %copy-start) | copy-done | bytes 536
  52.0 0.6 %slice.6 = f32[1,1,32]{2,1,0:T(1,128)} slice(f32[1,1,128]{2,1,0:T(1,128)S(1)} %bitcast.6), slice={[0:1], [0:1], [64:96]} | slice | bytes 256 | tf_op jit(solution)/shard_map/slice | solution.py:496
  52.6 0.5 copy.10
Async XLA Ops:
  51.4 0.6 %copy-start = (f32[1,128]{1,0:T(1,128)S(1)}, f32[1,128]{1,0:T(1,128)}, u32[]{:S(2)}) copy-start(f32[1,128]{1,0:T(1,128)} %late_interaction.1) | copy-start | bytes 1540

commit v4 on v3

--- a/solution.py
+++ b/solution.py
@@ -68,6 +68,20 @@
     own_rows = pl.ds(pl.multiple_of(rep * quarter, quarter), quarter)
     load_book = pltpu.make_async_copy(book_hbm, book.at[own_rows], local_sem.at[0])
     load_codes = pltpu.make_async_copy(code_hbm, codes, local_sem.at[1])
+    barrier = pltpu.get_barrier_semaphore()
+
+    def greet(dev):
+        pl.semaphore_signal(barrier, inc=1, device_id=dev, device_id_type=MESH)
+
+    def greet_line(k):
+        greet(at(z, near(y, k, n), c))
+        greet(at(z, near(y, k, n), 1 - c))
+        greet(at(near(z, k, n), y, c))
+
+    loop(1, n, lambda k: greet_line(n - k))
+    loop(1, nx, lambda k: greet({"shard": shard, "rep": near(rep, k, nx)}))
+    greet(sibling)
+
     small = [
         pltpu.make_async_copy(source, target, local_sem.at[4 + i])
         for i, (source, target) in enumerate((
@@ -79,21 +93,6 @@
         copy.start()
     load_book.start()
     load_codes.start()
-
-    barrier = pltpu.get_barrier_semaphore()
-
-    def greet(dev):
-        pl.semaphore_signal(barrier, inc=1, device_id=dev, device_id_type=MESH)
-
-    def greet_line(k):
-        greet(at(z, near(y, k, n), c))
-        greet(at(z, near(y, k, n), 1 - c))
-        greet(at(near(z, k, n), y, c))
-
-    loop(1, n, greet_line)
-    loop(1, nx, lambda k: greet({"shard": shard, "rep": near(rep, k, nx)}))
-    greet(sibling)
-
     for copy in small:
         copy.wait()
     toks[(z * CORES + c) * n + y] = query_ref[0:HALF]
@@ -124,7 +123,7 @@
         for copy in hop1_copies(k):
             copy.start()
 
-    loop(1, n, hop1_start)
+    loop(1, n, lambda k: hop1_start(n - k))
     loop(1, nx, lambda k: book_copy(k).start())
 
     load_codes.wait()
@@ -376,7 +375,7 @@
         merge1_copy(k, c).start()
         merge1_copy(k, 1 - c).start()
 
-    loop(1, n, merge1_start)
+    loop(1, n, lambda k: merge1_start(n - k))
     merge1_copy(0, 1 - c).start()
 
     def gathered(k):
@@ -408,7 +407,7 @@
         tz = near(z, k, n)
         return rcopy(line.at[pl.ds(tz, 1)], got2.at[pl.ds(z, 1)], sy.at[k], ry.at[z], at(tz, y, c))
 
-    loop(1, n, lambda k: merge2_copy(k).start())
+    loop(1, n, lambda k: merge2_copy(n - k).start())
 
     def merge1_sent(k):
         merge1_copy(k, c).wait_send()

time: 53.3 us -> 52.5 us (0.985)
  Pallas kernels: 50.8 us -> 50 us
    pallas_call x1, Pallas kernels: 50.8 us -> 50 us  [on_device(): pl.pallas_call(functools.partial(kernel, n, nx), out_shape=jax.ShapeDtype...]
where the time goes in v4:
time: 52.5 us; the launch traced here: 52.3 us
  Pallas kernels  50 us (95%)
  local copies, waits for them, and re-layouts  1.68 us (3%)
  between operations  0.65 us (1%)
    pallas_call x1, Pallas kernels, on_device(): pl.pallas_call(functools.partial(kernel, n, nx), out_shape=jax.ShapeDtype...  50 us
    unnamed x3, local copies, waits for them, and re-layouts  1.1 us

profile of v4, /device:TPU:1, one launch (start us, length us, event | category | flops | bytes accessed | tf_op | source)
XLA Modules:
  0.0 52.3 jit_solution(4548237823069437615)
XLA Ops:
  0.6 50.0 %late_interaction.1 = f32[1,128]{1,0:T(1,128)} custom-call(bf16[32,128]{1,0:T(8,128)(2,1)} %bitcast.4, s32[1,64]{1,0:T(1,128)} %bitcast.5, f32[4]{0:T(128)} %weight_hbm.1, s32[16]{0:T(128)} %length_hbm.1, s32[16,128]{1,0:T(8,128)} %id_hbm.1, bf16[1024,128]{1,0:T(8,128)(2,1)} %book_hbm.1, s32[16,128,128]{2,1,0:T(8,128)} %code_hbm.1), custom_call_target="tpu_custom_call" | custom-call | flops 4294967296 | bytes 2097152 | tf_op jit(solution)/shard_map/late_interaction/pallas_call | solution.py:444
  50.6 0.0 copy-start
  50.6 0.6 %copy-done = f32[1,128]{1,0:T(1,128)S(1)} copy-done((f32[1,128]{1,0:T(1,128)S(1)}, f32[1,128]{1,0:T(1,128)}, u32[]{:S(2)}) %copy-start) | copy-done | bytes 536
  51.2 0.6 %slice.6 = f32[1,1,32]{2,1,0:T(1,128)} slice(f32[1,1,128]{2,1,0:T(1,128)S(1)} %bitcast.6), slice={[0:1], [0:1], [64:96]} | slice | bytes 256 | tf_op jit(solution)/shard_map/slice | solution.py:495
  51.8 0.5 copy.10
Async XLA Ops:
  50.6 0.6 %copy-start = (f32[1,128]{1,0:T(1,128)S(1)}, f32[1,128]{1,0:T(1,128)}, u32[]{:S(2)}) copy-start(f32[1,128]{1,0:T(1,128)} %late_interaction.1) | copy-start | bytes 1540

commit v5 on v4

--- a/solution.py
+++ b/solution.py
@@ -281,28 +281,23 @@
         for u in range(pass_len):
             fetched[pl.ds(p * pass_len + u, 1)] = book32[pl.ds(id_ref[p, u], 1)]
 
-    loop(0, n_pass, fetch)
-
     def decode(p):
+        fetch(p)
         span = pl.ds(pl.multiple_of(p * pass_len, pass_len), pass_len)
         emb[span] = (fetched[span] + extra32[p]).astype(jnp.bfloat16)
 
     loop(0, n_pass, decode)
 
-    def last_quarter(h):
-        r = near(rep, nx - 1, nx)
-        for t in range(n):
-            tile = h * n + t
-            best_acc[tile] = jnp.maximum(best_acc[tile], best_of(tile, r))
-
-    loop(0, 2, last_quarter)
+    last = near(rep, nx - 1, nx)
+    for tile in range(2 * n):
+        best_acc[tile] = jnp.maximum(best_acc[tile], best_of(tile, last))
     to_smem.wait()
 
     slot_iota = lax.broadcasted_iota(jnp.int32, (pass_len, SLOTS * 2 * HALF), 0)
 
     def score(i):
-        for u in range(4):
-            p = i * 4 + u
+        for u in range(8):
+            p = i * 8 + u
             parts = []
             for k in range(SLOTS):
                 parts.append(toks[jnp.clip(slot_smem[p, k], 0, n_blocks - 1)])
@@ -317,7 +312,7 @@
             similar = jnp.where(slot_iota < length_ref[p], similar, FAR_BELOW)
             pair_best[pl.ds(p, 1)] = jnp.max(similar, axis=0, keepdims=True)
 
-    loop(0, n_pass // 4, score)
+    loop(0, n_pass // 8, score)
 
     tok_of = lax.broadcasted_iota(jnp.int32, (SLOTS * 2 * HALF, 128), 0) >> 5
     col_of = lax.broadcasted_iota(jnp.int32, (SLOTS * 2 * HALF, 128), 1)
@@ -347,6 +342,14 @@
             return part
         return jnp.concatenate([part, jnp.full((n, 128 - lane_half), FAR_BELOW, jnp.float32)], axis=1)
 
+    me = c * n + y
+
+    def merge1_copy(k, c_):
+        ty = near(y, k, n)
+        return rcopy(
+            tiles.at[c_ * n + ty], got1.at[me], sx.at[c_ * n + ty], rx.at[me], at(z, ty, c_)
+        )
+
     for c_ in range(CORES):
         cols = slice(c_ * lane_half, (c_ + 1) * lane_half)
         best_a = fit(best[0:n, cols])
@@ -362,21 +365,8 @@
             t = c_ * n + y_
             tile = chosen[t * n : (t + 1) * n]
             tiles[t] = jnp.where(in_a, part_a, jnp.where(in_b, part_b, tile))
-
-    me = c * n + y
-
-    def merge1_copy(k, c_):
-        ty = near(y, k, n)
-        return rcopy(
-            tiles.at[c_ * n + ty], got1.at[me], sx.at[c_ * n + ty], rx.at[me], at(z, ty, c_)
-        )
-
-    def merge1_start(k):
-        merge1_copy(k, c).start()
-        merge1_copy(k, 1 - c).start()
-
-    loop(1, n, lambda k: merge1_start(n - k))
-    merge1_copy(0, 1 - c).start()
+        loop(1, n, lambda k: merge1_copy(n - k, c_).start())
+        pl.when(c != c_)(lambda: merge1_copy(0, c_).start())
 
     def gathered(k):
         for copy in hop1_copies(k) + hop2_copies(k):

time: 52.5 us -> 52.2 us (level)
  no operation moved by 1% of the time
where the time goes in v5:
time: 52.2 us; the launch traced here: 52.1 us
  Pallas kernels  49.7 us (95%)
  local copies, waits for them, and re-layouts  1.68 us (3%)
  between operations  0.65 us (1%)
    pallas_call x1, Pallas kernels, on_device(): pl.pallas_call(functools.partial(kernel, n, nx), out_shape=jax.ShapeDtype...  49.7 us
    unnamed x3, local copies, waits for them, and re-layouts  1.1 us

profile of v5, /device:TPU:1, one launch (start us, length us, event | category | flops | bytes accessed | tf_op | source)
XLA Modules:
  0.0 52.1 jit_solution(5835284504267847129)
XLA Ops:
  0.6 49.7 %late_interaction.1 = f32[1,128]{1,0:T(1,128)} custom-call(bf16[32,128]{1,0:T(8,128)(2,1)} %bitcast.4, s32[1,64]{1,0:T(1,128)} %bitcast.5, f32[4]{0:T(128)} %weight_hbm.1, s32[16]{0:T(128)} %length_hbm.1, s32[16,128]{1,0:T(8,128)} %id_hbm.1, bf16[1024,128]{1,0:T(8,128)(2,1)} %book_hbm.1, s32[16,128,128]{2,1,0:T(8,128)} %code_hbm.1), custom_call_target="tpu_custom_call" | custom-call | flops 4294967296 | bytes 2097152 | tf_op jit(solution)/shard_map/late_interaction/pallas_call | solution.py:434
  50.4 0.0 copy-start
  50.4 0.6 %copy-done = f32[1,128]{1,0:T(1,128)S(1)} copy-done((f32[1,128]{1,0:T(1,128)S(1)}, f32[1,128]{1,0:T(1,128)}, u32[]{:S(2)}) %copy-start) | copy-done | bytes 536
  51.0 0.6 %slice.6 = f32[1,1,32]{2,1,0:T(1,128)} slice(f32[1,1,128]{2,1,0:T(1,128)S(1)} %bitcast.6), slice={[0:1], [0:1], [64:96]} | slice | bytes 256 | tf_op jit(solution)/shard_map/slice | solution.py:485
  51.6 0.5 copy.10
Async XLA Ops:
  50.4 0.6 %copy-start = (f32[1,128]{1,0:T(1,128)S(1)}, f32[1,128]{1,0:T(1,128)}, u32[]{:S(2)}) copy-start(f32[1,128]{1,0:T(1,128)} %late_interaction.1) | copy-start | bytes 1540
